TPU v7x, 512 devices: a whole 4x8x8 slice. The times are simulated.
512 devices in a mesh: depth: 16 (over x, z_lo), chan: 32 (over y, z_hi, core).
Axes of the slice: x: 4, y: 8, z: 8 (z_hi: 2, z_lo: 4; z = z_hi * 4 + z_lo), core: 2. Of those that a mesh axis runs over, the one named last changes fastest.
Arguments:
- volume: bfloat16 [16, 16, 16, 1024], P('depth', None, None, 'chan'), may hold values from -6 to 6
- cotangent: bfloat16 [16, 16, 16, 1024], P('depth', None, None, 'chan'), may hold values from -6 to 6
- kernel: bfloat16 [1024, 27, 1024], P('chan'), may hold values from -0.0390625 to 0.0390625
Outputs:
- input_grad: bfloat16 [16, 16, 16, 1024], P('depth', None, None, 'chan')
- kernel_grad: float32 [32, 32, 27, 1024], P('chan', None, None, 'depth')
All inputs are finite; a program needn't handle non-finite values.
Results may differ from a plain program's by a relative error of at most 0.023.
Values may be sent and summed in bfloat16 or wider, within the bound.
A program may use at most 64 MiB of HBM per device.

v0:
```python
import jax
import jax.numpy as jnp
from jax import lax
from jax.sharding import PartitionSpec as P


def extended(block, sides, width):
    for axis, dim in sides:
        count = lax.axis_size(axis)
        forward = [(i, i + 1) for i in range(count - 1)]
        backward = [(target, source) for source, target in forward]
        low = lax.ppermute(
            lax.slice_in_dim(block, block.shape[dim] - width, None, axis=dim), axis, forward
        )
        high = lax.ppermute(lax.slice_in_dim(block, 0, width, axis=dim), axis, backward)
        block = jnp.concatenate([low, block, high], axis=dim)
    return block


def passed_along(value, axis, steps):
    count = lax.axis_size(axis)
    first, last = (max(0, -steps), min(count, count - steps))
    return lax.ppermute(value, axis, [(source, source + steps) for source in range(first, last)])


def tap_offsets():
    return [(a, b, c) for a in range(3) for b in range(3) for c in range(3)]


def tap_window(padded, a, b, c, planes, height, width):
    chans = padded.shape[3]
    return padded[a : a + planes, b : b + height, c : c + width, :].reshape(
        planes * height * width, chans
    )


def local(volume, cotangent, kernel):
    planes, height, width, shard = volume.shape
    chans = kernel.shape[2]
    rows = planes * height * width
    framed = extended(volume, (("depth", 0),), 1)
    whole = lax.all_gather(framed, "chan", axis=3, tiled=True)
    padded = jnp.pad(whole, ((0, 0), (1, 1), (1, 1), (0, 0)))
    pre = jnp.zeros((rows, shard), jnp.float32)
    for tap, (a, b, c) in enumerate(tap_offsets()):
        window = tap_window(padded, a, b, c, planes, height, width)
        pre = pre + lax.dot_general(
            window, kernel[:, tap, :], (((1,), (1,)), ((), ())), preferred_element_type=jnp.float32
        )
    sig = jax.nn.sigmoid(pre)
    grad_out = cotangent.reshape(rows, shard).astype(jnp.float32)
    slope = (grad_out * sig * (1.0 + pre * (1.0 - sig))).astype(jnp.bfloat16)
    parts = [
        lax.dot_general(
            slope,
            tap_window(padded, a, b, c, planes, height, width),
            (((0,), (0,)), ((), ())),
            preferred_element_type=jnp.float32,
        )
        for a, b, c in tap_offsets()
    ]
    stacked = jnp.stack(parts, 1).reshape(1, shard, 27, chans)
    kernel_grad = lax.psum_scatter(
        stacked.astype(jnp.bfloat16), "depth", scatter_dimension=3, tiled=True
    ).astype(jnp.float32)
    slope_vol = slope.reshape(planes, height, width, shard)
    taps_t = jnp.transpose(kernel, (1, 0, 2)).reshape(27 * shard, chans)
    spread = jnp.pad(slope_vol, ((2, 2), (1, 1), (1, 1), (0, 0)))
    extent = planes + 2
    columns = jnp.concatenate(
        [
            spread[2 - a : 2 - a + extent, 2 - b : 2 - b + height, 2 - c : 2 - c + width, :]
            for a, b, c in tap_offsets()
        ],
        axis=3,
    ).reshape(extent * height * width, 27 * shard)
    wide = jnp.dot(columns, taps_t, preferred_element_type=jnp.float32).reshape(
        extent, height, width, chans
    )
    from_below = passed_along(wide[extent - 1].astype(jnp.bfloat16), "depth", 1).astype(jnp.float32)
    from_above = passed_along(wide[0].astype(jnp.bfloat16), "depth", -1).astype(jnp.float32)
    inner = wide[1 : extent - 1]
    inner = inner.at[0].add(from_below)
    inner = inner.at[planes - 1].add(from_above)
    input_grad = lax.psum_scatter(
        inner.astype(jnp.bfloat16), "chan", scatter_dimension=3, tiled=True
    )
    return (input_grad, kernel_grad)


def solution(mesh):
    return jax.shard_map(
        local,
        mesh=mesh,
        in_specs=(
            P("depth", None, None, "chan"),
            P("depth", None, None, "chan"),
            P("chan", None, None),
        ),
        out_specs=(P("depth", None, None, "chan"), P("chan", None, None, "depth")),
        check_vma=False,
    )
```

profile of v0, /device:TPU:8, one launch (start us, length us, event | category | flops | bytes accessed | tf_op | source)
XLA Modules:
  0.0 497.6 jit_solution(6101028641297577007)
XLA Ops:
  7.2 1.0 copy.13
  8.2 4.3 collective-permute-start
  12.5 1.3 collective-permute-start.1
  13.8 1.4 collective-permute-done
  15.2 7.2 %collective-permute-done.1 = bf16[1,16,16,32]{2,1,0,3:T(8,128)(2,1)S(1)} collective-permute-done((bf16[1,16,16,32]{2,1,0,3:T(8,128)(2,1)S(1)}, bf16[1,16,16,32]{2,1,0,3:T(8,128)(2,1)S(1)}, u32[]{:S(2)}, u32[]{:S(2)}) %collective-permute-start.1) | collective-permute-done | bytes 16416 | tf_op jit(solution)/shard_map/ppermute | solution.py:15
  22.4 0.8 pad_maximum_fusion
  23.3 0.9 bitcast_convert_fusion
  24.2 165.2 %all-gather.2.cloned.1.call-done = bf16[3,16,16,1024]{2,1,0,3:T(8,128)(2,1)} async-done(((bf16[3,16,16,32]{2,1,0,3:T(8,128)(2,1)}), bf16[3,16,16,1024]{2,1,0,3:T(8,128)(2,1)}) %all-gather.2.cloned.1.call-update) | async-done | bytes 1572880 | tf_op jit(solution)/shard_map/all_gather | solution.py:42
  189.4 12.1 %copy.16 = bf16[3,16,16,1024]{3,2,1,0:T(8,128)(2,1)S(1)} copy(bf16[3,16,16,1024]{2,1,0,3:T(8,128)(2,1)} %all-gather.2.cloned.1.call-done) | data formatting | bytes 3145728 | tf_op jit(solution)/shard_map/all_gather | solution.py:42
  201.5 3.4 pad_slice_fusion
  205.8 2.1 copy-done.47
  216.3 2.5 pad_slice_fusion.24
  218.8 2.5 pad_slice_fusion.25
  225.4 6.3 %concatenate.19 = bf16[3,16,16,864]{3,2,1,0:T(8,128)(2,1)} concatenate(bf16[3,16,16,32]{3,2,1,0:T(8,128)(2,1)} %get-tuple-element.81, bf16[3,16,16,32]{3,2,1,0:T(8,128)(2,1)} %get-tuple-element.56, bf16[3,16,16,32]{3,2,1,0:T(8,128)(2,1)} %get-tuple-element.57, bf16[3,16,16,32]{3,2,1,0:T(8,128)(2,1)} %get-tuple-element.58, bf16[3,16,16,32]{3,2,1,0:T(8,128)(2,1)} %get-tuple-element.59, ...), dimensions={3} | concatenate | bytes 2654208 | tf_op jit(solution)/shard_map/concatenate | solution.py:70
  231.7 3.7 fusion.113
  235.5 1.5 collective-permute-start.2
  237.0 1.5 collective-permute-start.3
  239.2 9.6 %collective-permute-done.2 = bf16[16,16,1024]{2,1,0:T(8,128)(2,1)S(1)} collective-permute-done((bf16[16,16,1024]{2,1,0:T(8,128)(2,1)S(1)}, bf16[16,16,1024]{2,1,0:T(8,128)(2,1)S(1)}, u32[]{:S(2)}, u32[]{:S(2)}) %collective-permute-start.2) | collective-permute-done | bytes 524320 | tf_op jit(solution)/shard_map/ppermute | solution.py:23
  248.8 15.4 %collective-permute-done.3 = bf16[16,16,1024]{2,1,0:T(8,128)(2,1)S(1)} collective-permute-done((bf16[16,16,1024]{2,1,0:T(8,128)(2,1)S(1)}, bf16[16,16,1024]{2,1,0:T(8,128)(2,1)S(1)}, u32[]{:S(2)}, u32[]{:S(2)}) %collective-permute-start.3) | collective-permute-done | bytes 524320 | tf_op jit(solution)/shard_map/ppermute | solution.py:23
  264.5 4.7 copy.22
  269.1 6.2 %reshape.648 = bf16[1024,256]{1,0:T(8,128)(2,1)} reshape(bf16[1024,1,16,16]{3,2,1,0:T(8,128)(2,1)} %bitcast.322) | data formatting | bytes 1048576
  275.5 0.8 fusion.47
  276.3 0.8 fusion.49
  277.1 0.8 fusion.51
  277.9 0.8 fusion.53
  278.7 12.7 %copy.24 = bf16[1,32,27,1024]{1,2,0,3:T(8,128)(2,1)} copy(bf16[1,32,27,1024]{3,1,2,0:T(8,128)(2,1)} %fusion.53) | data formatting | bytes 3538944
  291.4 10.9 %reshape.650 = bf16[1024,864]{1,0:T(8,128)(2,1)} reshape(bf16[1024,1,27,32]{3,2,1,0:T(8,128)(2,1)} %bitcast.321) | data formatting | bytes 3538944
  302.3 93.1 %reduce-scatter.7.cloned.1.call-done = bf16[32,256]{1,0:T(8,128)(2,1)} async-done(((bf16[1024,256]{1,0:T(8,128)(2,1)}), bf16[32,256]{1,0:T(8,128)(2,1)}) %reduce-scatter.7.cloned.1.call-update) | async-done | bytes 16400
  395.4 0.9 reshape.649
  397.1 91.3 %reduce-scatter.9.cloned.1.call-done = bf16[64,864]{1,0:T(8,128)(2,1)} async-done(((bf16[1024,864]{1,0:T(8,128)(2,1)}), bf16[64,864]{1,0:T(8,128)(2,1)}) %reduce-scatter.9.cloned.1.call-update) | async-done | bytes 110608
  488.4 1.3 reshape.651
  490.2 0.8 convert_element_type.54
  (161 shorter events, 15.0 us)
Async XLA Ops:
  7.2 182.2 %all-gather.2.cloned.1.call-start = ((), (), s32[]{:S(2)}) async-start(), calls=%async_computation.2 | async-start | bytes 12976128 | tf_op jit(solution)/shard_map/all_gather | solution.py:42
  8.2 7.0 %collective-permute-start = (bf16[1,16,16,32]{2,1,0,3:T(8,128)(2,1)S(1)}, bf16[1,16,16,32]{2,1,0,3:T(8,128)(2,1)S(1)}, u32[]{:S(2)}, u32[]{:S(2)}) collective-permute-start(bf16[1,16,16,32]{2,1,0,3:T(8,128)(2,1)S(1)} %copy.13), channel_id=1, source_target_pairs={{0,32},{32,64},{64,96},{96,128},{128,160},{160,192},{192,224},{224... | collective-permute-start | bytes 49160 | tf_op jit(solution)/shard_map/ppermute | solution.py:12
  12.5 9.9 %collective-permute-start.1 = (bf16[1,16,16,32]{2,1,0,3:T(8,128)(2,1)S(1)}, bf16[1,16,16,32]{2,1,0,3:T(8,128)(2,1)S(1)}, u32[]{:S(2)}, u32[]{:S(2)}) collective-permute-start(bf16[1,16,16,32]{2,1,0,3:T(8,128)(2,1)S(1)} %copy.13), channel_id=1, source_target_pairs={{32,0},{64,32},{96,64},{128,96},{160,128},{192,160},{224,192},{256... | collective-permute-start | bytes 49160 | tf_op jit(solution)/shard_map/ppermute | solution.py:15
  23.3 372.1 %reduce-scatter.7.cloned.1.call-start = ((), (), s32[]{:S(2)}) async-start(), calls=%async_computation.3 | async-start | bytes 540672
  204.9 3.8 copy-start.38
  204.9 4.3 copy-start.36
  204.9 4.6 copy-start.40
  205.0 4.6 copy-start.42
  205.0 4.6 copy-start.34
  205.0 4.8 copy-start.32
  205.0 5.1 %copy-start.30 = (bf16[1,16,16,1024]{3,2,1,0:T(8,128)(2,1)}, bf16[1,16,16,1024]{3,2,1,0:T(8,128)(2,1)S(1)}, u32[]{:S(2)}) copy-start(bf16[1,16,16,1024]{3,2,1,0:T(8,128)(2,1)S(1)} %get-tuple-element.35) | copy-start | bytes 1572868
  205.0 5.4 %copy-start.28 = (bf16[1,16,16,1024]{3,2,1,0:T(8,128)(2,1)}, bf16[1,16,16,1024]{3,2,1,0:T(8,128)(2,1)S(1)}, u32[]{:S(2)}) copy-start(bf16[1,16,16,1024]{3,2,1,0:T(8,128)(2,1)S(1)} %get-tuple-element.36) | copy-start | bytes 1572868
  205.0 5.6 %copy-start.26 = (bf16[1,16,16,1024]{3,2,1,0:T(8,128)(2,1)}, bf16[1,16,16,1024]{3,2,1,0:T(8,128)(2,1)S(1)}, u32[]{:S(2)}) copy-start(bf16[1,16,16,1024]{3,2,1,0:T(8,128)(2,1)S(1)} %get-tuple-element.37) | copy-start | bytes 1572868
  205.0 5.9 %copy-start.24 = (bf16[1,16,16,1024]{3,2,1,0:T(8,128)(2,1)}, bf16[1,16,16,1024]{3,2,1,0:T(8,128)(2,1)S(1)}, u32[]{:S(2)}) copy-start(bf16[1,16,16,1024]{3,2,1,0:T(8,128)(2,1)S(1)} %get-tuple-element.38) | copy-start | bytes 1572868
  205.0 6.2 %copy-start.22 = (bf16[1,16,16,1024]{3,2,1,0:T(8,128)(2,1)}, bf16[1,16,16,1024]{3,2,1,0:T(8,128)(2,1)S(1)}, u32[]{:S(2)}) copy-start(bf16[1,16,16,1024]{3,2,1,0:T(8,128)(2,1)S(1)} %get-tuple-element.39) | copy-start | bytes 1572868
  205.0 6.7 %copy-start.20 = (bf16[1,16,16,1024]{3,2,1,0:T(8,128)(2,1)}, bf16[1,16,16,1024]{3,2,1,0:T(8,128)(2,1)S(1)}, u32[]{:S(2)}) copy-start(bf16[1,16,16,1024]{3,2,1,0:T(8,128)(2,1)S(1)} %get-tuple-element.40) | copy-start | bytes 1572868
  205.0 7.0 %copy-start.18 = (bf16[1,16,16,1024]{3,2,1,0:T(8,128)(2,1)}, bf16[1,16,16,1024]{3,2,1,0:T(8,128)(2,1)S(1)}, u32[]{:S(2)}) copy-start(bf16[1,16,16,1024]{3,2,1,0:T(8,128)(2,1)S(1)} %get-tuple-element.41) | copy-start | bytes 1572868
  205.1 7.3 %copy-start.16 = (bf16[1,16,16,1024]{3,2,1,0:T(8,128)(2,1)}, bf16[1,16,16,1024]{3,2,1,0:T(8,128)(2,1)S(1)}, u32[]{:S(2)}) copy-start(bf16[1,16,16,1024]{3,2,1,0:T(8,128)(2,1)S(1)} %get-tuple-element.42) | copy-start | bytes 1572868
  205.1 7.5 %copy-start.14 = (bf16[1,16,16,1024]{3,2,1,0:T(8,128)(2,1)}, bf16[1,16,16,1024]{3,2,1,0:T(8,128)(2,1)S(1)}, u32[]{:S(2)}) copy-start(bf16[1,16,16,1024]{3,2,1,0:T(8,128)(2,1)S(1)} %get-tuple-element.43) | copy-start | bytes 1572868
  205.1 7.8 %copy-start.12 = (bf16[1,16,16,1024]{3,2,1,0:T(8,128)(2,1)}, bf16[1,16,16,1024]{3,2,1,0:T(8,128)(2,1)S(1)}, u32[]{:S(2)}) copy-start(bf16[1,16,16,1024]{3,2,1,0:T(8,128)(2,1)S(1)} %get-tuple-element.44) | copy-start | bytes 1572868
  205.1 8.1 %copy-start.10 = (bf16[1,16,16,1024]{3,2,1,0:T(8,128)(2,1)}, bf16[1,16,16,1024]{3,2,1,0:T(8,128)(2,1)S(1)}, u32[]{:S(2)}) copy-start(bf16[1,16,16,1024]{3,2,1,0:T(8,128)(2,1)S(1)} %get-tuple-element.45) | copy-start | bytes 1572868
  205.1 8.3 %copy-start.8 = (bf16[1,16,16,1024]{3,2,1,0:T(8,128)(2,1)}, bf16[1,16,16,1024]{3,2,1,0:T(8,128)(2,1)S(1)}, u32[]{:S(2)}) copy-start(bf16[1,16,16,1024]{3,2,1,0:T(8,128)(2,1)S(1)} %get-tuple-element.46) | copy-start | bytes 1572868
  205.1 10.0 %copy-start.44 = (bf16[1,16,16,1024]{3,2,1,0:T(8,128)(2,1)}, bf16[1,16,16,1024]{3,2,1,0:T(8,128)(2,1)S(1)}, u32[]{:S(2)}) copy-start(bf16[1,16,16,1024]{3,2,1,0:T(8,128)(2,1)S(1)} %get-tuple-element.28) | copy-start | bytes 1572868
  205.8 3.8 copy-start.6
  205.8 5.7 %copy-start.4 = (bf16[1,16,16,1024]{3,2,1,0:T(8,128)(2,1)}, bf16[1,16,16,1024]{3,2,1,0:T(8,128)(2,1)S(1)}, u32[]{:S(2)}) copy-start(bf16[1,16,16,1024]{3,2,1,0:T(8,128)(2,1)S(1)} %get-tuple-element.52) | copy-start | bytes 1572868
  205.8 7.9 %copy-start.2 = (bf16[1,16,16,1024]{3,2,1,0:T(8,128)(2,1)}, bf16[1,16,16,1024]{3,2,1,0:T(8,128)(2,1)S(1)}, u32[]{:S(2)}) copy-start(bf16[1,16,16,1024]{3,2,1,0:T(8,128)(2,1)S(1)} %get-tuple-element.48) | copy-start | bytes 1572868
  205.8 8.2 %copy-start = (bf16[1,16,16,1024]{3,2,1,0:T(8,128)(2,1)}, bf16[1,16,16,1024]{3,2,1,0:T(8,128)(2,1)S(1)}, u32[]{:S(2)}) copy-start(bf16[1,16,16,1024]{3,2,1,0:T(8,128)(2,1)S(1)} %get-tuple-element.51) | copy-start | bytes 1572868
  216.3 5.0 %copy-start.43 = (bf16[1,16,16,1024]{3,2,1,0:T(8,128)(2,1)S(1)}, bf16[1,16,16,1024]{3,2,1,0:T(8,128)(2,1)}, u32[]{:S(2)}) copy-start(bf16[1,16,16,1024]{3,2,1,0:T(8,128)(2,1)} %copy-done.42) | copy-start | bytes 1572868
  235.5 13.3 %collective-permute-start.2 = (bf16[16,16,1024]{2,1,0:T(8,128)(2,1)S(1)}, bf16[16,16,1024]{2,1,0:T(8,128)(2,1)S(1)}, u32[]{:S(2)}, u32[]{:S(2)}) collective-permute-start(bf16[16,16,1024]{2,1,0:T(8,128)(2,1)S(1)} %bitcast.385), channel_id=1, source_target_pairs={{0,32},{32,64},{64,96},{96,128},{128,160},{160,192},{192,224},{224... | collective-permute-start | bytes 1572872 | tf_op jit(solution)/shard_map/ppermute | solution.py:23
  237.0 27.2 %collective-permute-start.3 = (bf16[16,16,1024]{2,1,0:T(8,128)(2,1)S(1)}, bf16[16,16,1024]{2,1,0:T(8,128)(2,1)S(1)}, u32[]{:S(2)}, u32[]{:S(2)}) collective-permute-start(bf16[16,16,1024]{2,1,0:T(8,128)(2,1)S(1)} %bitcast.384), channel_id=1, source_target_pairs={{32,0},{64,32},{96,64},{128,96},{160,128},{192,160},{224,192},{256... | collective-permute-start | bytes 1572872 | tf_op jit(solution)/shard_map/ppermute | solution.py:23
  239.2 25.0 %copy-start.46 = (bf16[1,32,27,1024]{3,1,2,0:T(8,128)(2,1)}, bf16[1,32,27,1024]{3,1,2,0:T(8,128)(2,1)S(1)}, u32[]{:S(2)}) copy-start(bf16[1,32,27,1024]{3,1,2,0:T(8,128)(2,1)S(1)} %fusion.45) | copy-start | bytes 5308420
  275.4 213.0 %reduce-scatter.9.cloned.1.call-start = ((), (), s32[]{:S(2)}) async-start(), calls=%async_computation.4 | async-start | bytes 1949696
  (24 other events, 46.0 us)
Sparse Core Ops, SparseCore 0:
  23.4 165.9 all-gather.1
  275.5 119.8 reduce-scatter.6
  398.5 89.8 reduce-scatter.8
where the time goes:
time: 499 us; the launch traced here: 498 us
  waiting for transfers between devices  383 us (77%)
  local copies, waits for them, and re-layouts  69.8 us (14%)
  matrix products  18.2 us (4%)
  between operations  15 us (3%)
  starting transfers between devices  8.62 us (2%)
    unnamed x5, waiting for transfers between devices  184 us
    all_gather x1, waiting for transfers between devices, local(): whole = lax.all_gather(framed, 'chan', axis=3, tiled=True)  165 us
    unnamed x107, local copies, waits for them, and re-layouts  42 us
    ppermute x2, waiting for transfers between devices, passed_along(): lax.ppermute(value, axis, [(source, source + steps) for source in range(f...  25 us
    all_gather x1, local copies, waits for them, and re-layouts, local(): whole = lax.all_gather(framed, 'chan', axis=3, tiled=True)  12.1 us
  transfers between devices with their start and end apart: 7, of which 7 were waited for; matrix products, arithmetic and copies ran while one was open for 6% of the time, Pallas kernels for 0%

commit v1 on v0

v1 whole, which is shorter than its diff:
```python
import functools

import jax
import jax.numpy as jnp
from jax import lax
from jax.experimental import pallas as pl
from jax.experimental.pallas import tpu as pltpu
from jax.sharding import PartitionSpec as P

MESH = pl.DeviceIdType.MESH
F32, BF16 = jnp.float32, jnp.bfloat16
ND, NX, NL, NZ, NK = 16, 4, 4, 8, 32
CS, SIDE, VOX, CH = 32, 16, 256, 1024
HALF, TAPS, O2 = 512, 27, 64
TROWS, TPAD = TAPS * O2, 28 * O2


def kernel_body(
    vol_hbm, cot_hbm, k_hbm, ig_ref, kg_ref,
    vin, cin, xt, xh, kx, ktmp, k2, kt, psend, prec, sl, ss, cm, og, rs, v2, xc, slb, acc,
    in_sem, k_send, k_recv, a_send, a_recv, p_send, p_recv, s_send, s_recv, n_send, n_recv,
    v_send, v_recv, f_send, r_send, r_recv,
):
    d, k = lax.axis_index("depth"), lax.axis_index("chan")
    x, zl = d // NL, d % NL
    y, zh, c, m = k // 4, (k // 2) % 2, k % 2, k // 2
    z, sib = zh * NL + zl, k + 1 - 2 * c
    khalf = k // 16
    self_a = khalf == c
    self_v = jnp.logical_and(zl % 2 == c, x // 2 == c)

    def remote(src, dst, ssem, rsem, dev):
        return pltpu.make_async_remote_copy(
            src_ref=src, dst_ref=dst, send_sem=ssem, recv_sem=rsem, device_id=dev,
            device_id_type=MESH,
        )

    def taken(ref, sem):
        pltpu.make_async_copy(ref, ref, sem).wait()

    vol_in = pltpu.make_async_copy(vol_hbm, vin, in_sem.at[0])
    cot_in = pltpu.make_async_copy(cot_hbm, cin, in_sem.at[1])
    k_in = pltpu.make_async_copy(
        k_hbm.at[:, :, pl.ds(pl.multiple_of(c * HALF, HALF), HALF)], kx.at[0], in_sem.at[2]
    )
    vol_in.start()
    cot_in.start()
    k_in.start()

    bar = pltpu.get_barrier_semaphore()

    def greet(dd, kk):
        pl.semaphore_signal(bar, inc=1, device_id=(dd, kk), device_id_type=MESH)

    @pl.loop(0, 16)
    def _(j):
        to, frm = 2 * j + khalf, 16 * c + j

        @pl.when(to != k)
        def _():
            greet(d, to)

        @pl.when(frm != k)
        def _():
            greet(d, frm)

    @pl.loop(1, ND)
    def _(j):
        greet((d + j) % ND, k)

    greet(d, sib)
    greet((d + 1) % ND, sib)
    greet((d + ND - 1) % ND, sib)
    odd = (z + c) % 2

    @pl.loop(0, 8)
    def _(j):
        xs, t = j // 2, j % 2
        step = jnp.where(odd == 1, 2 * t - 1, t * (2 - 4 * (xs % 2)))
        zs = (z - step + NZ) % NZ
        dd, kk = xs * NL + zs % NL, (y * 2 + zs // NL) * 2 + x // 2

        @pl.when(jnp.logical_or(dd != d, kk != k))
        def _():
            greet(dd, kk)

    vol_in.wait()
    xt[...] = vin[...].astype(F32).T.astype(BF16)

    zero = jnp.zeros((CS, VOX), BF16)
    slb[0] = jnp.zeros((3 * CS, VOX), BF16)
    slb[ND + 1] = jnp.zeros((3 * CS, VOX), BF16)
    sl[0] = zero
    sl[ND + 1] = zero
    cm[pl.ds(TROWS, O2), :] = jnp.zeros((O2, VOX), BF16)
    k2[pl.ds(TROWS, O2), :] = jnp.zeros((O2, HALF), BF16)

    @pl.when(d == 0)
    def _():
        prec[0] = jnp.zeros((2, CS, VOX), F32)
        ss[0] = zero

    @pl.when(d == ND - 1)
    def _():
        prec[2] = jnp.zeros((2, CS, VOX), F32)
        ss[2] = zero

    sa, sv = self_a.astype(jnp.int32), self_v.astype(jnp.int32)
    pl.semaphore_wait(bar, 2 * (16 - sa) + 15 + 3 + 8 - sv)

    a_slot = xh.at[pl.ds(pl.multiple_of((k % 16) * CS, CS), CS)]

    @pl.loop(0, 16)
    def _(j):
        to = 2 * ((m + j + 8) % 16) + khalf

        @pl.when(to != k)
        def _():
            remote(xt, a_slot, a_send, a_recv, (d, to)).start()

        @pl.when(to == k)
        def _():
            pltpu.make_async_copy(xt, a_slot, a_recv).start()

    k_out = remote(
        k_hbm.at[:, :, pl.ds(pl.multiple_of((1 - c) * HALF, HALF), HALF)], kx.at[1], k_send, k_recv,
        (d, sib),
    )
    k_out.start()

    def widen(r):
        @pl.loop(0, CS)
        def _(o):
            rows = kx[r, o].astype(F32)
            for g in range(4):
                ktmp[g, pl.ds(pl.multiple_of((r * CS + o) * 32, 32), TAPS), :] = rows[
                    :, g * 128 : g * 128 + 128
                ]

    k_in.wait()
    widen(0)
    k_out.wait_recv()
    widen(1)
    for t in range(TAPS):
        for g in range(4):
            k2[pl.ds(t * O2, O2), pl.ds(g * 128, 128)] = ktmp.at[g][
                pl.ds(t, O2, stride=32), :
            ].astype(BF16)
    for p in range(14):
        kt[:, pl.ds(p * 128, 128)] = k2[pl.ds(p * 128, 128), :].T

    lane = lax.broadcasted_iota(jnp.int32, (1, VOX), 1)
    hh, ww = lane // SIDE, lane % SIDE
    h_lo, h_hi = hh >= 1, hh <= SIDE - 2
    w_lo, w_hi = ww >= 1, ww <= SIDE - 2

    def moved(v, step, keep):
        return jnp.where(keep, pltpu.roll(v, step % VOX, 1), 0.0)

    def up(v):
        return moved(v, SIDE, h_lo)

    def down(v):
        return moved(v, -SIDE, h_hi)

    def right(v):
        return moved(v, 1, w_lo)

    def left(v):
        return moved(v, -1, w_hi)

    cin_t = None
    taken(xh, a_recv)
    xv = xh[...]

    for a in (0, 2, 1):
        yv = jnp.dot(k2[pl.ds(a * 9 * O2, 9 * O2), :], xv, preferred_element_type=F32)

        def tap(b, cc):
            at = (b * 3 + cc) * O2
            return yv[at : at + O2, :]

        cols = [tap(1, cc) + up(tap(0, cc)) + down(tap(2, cc)) for cc in range(3)]
        tot = cols[1] + right(cols[0]) + left(cols[2])
        psend[a, 0] = tot[:CS]
        psend[a, 1] = tot[CS:]
        if a == 1:
            remote(psend.at[1, 1], prec.at[1, c], p_send.at[2], p_recv.at[1, c], (d, sib)).start()
        else:
            i = 0 if a == 0 else 1
            there = d + 1 - a

            @pl.when(jnp.logical_and(there >= 0, there < ND))
            def _():
                for r, kk in ((0, k), (1, sib)):
                    remote(
                        psend.at[a, r], prec.at[a, c], p_send.at[3 + 2 * i + r], p_recv.at[a, c],
                        (there, kk),
                    ).start()

    @pl.loop(0, 8)
    def _(j):
        xd, t = 2 * c + j // 4, j % 4
        step = jnp.where(t == 3, 2 - 4 * (x % 2), t - 1)
        zd = (z + step + NZ) % NZ
        dd, kk = xd * NL + zd % NL, (y * 2 + zd // NL) * 2 + zl % 2
        src = xh.at[pl.ds(pl.multiple_of(((j // 4) * NL + zd % NL) * 64, 64), 64)]
        own = jnp.logical_and(dd == d, kk == k)

        @pl.when(jnp.logical_not(own))
        def _():
            remote(src, v2.at[d], v_send, v_recv.at[d], (dd, kk)).start()

        @pl.when(own)
        def _():
            pltpu.make_async_copy(src, v2.at[d], v_recv.at[d]).start()

    cot_in.wait()
    cot_t = cin[...].astype(F32).T
    not_first, not_last = d >= 1, d <= ND - 2
    taken(prec.at[1, 1 - c], p_recv.at[1, 1 - c])

    @pl.when(not_first)
    def _():
        taken(prec.at[0, 0], p_recv.at[0, 0])
        taken(prec.at[0, 1], p_recv.at[0, 1])

    @pl.when(not_last)
    def _():
        taken(prec.at[2, 0], p_recv.at[2, 0])
        taken(prec.at[2, 1], p_recv.at[2, 1])

    pre = psend[1, 0] + prec[1, 1 - c]
    pre = pre + (prec[0, 0] + prec[0, 1]) + (prec[2, 0] + prec[2, 1])
    sig = 1.0 / (1.0 + jnp.exp(-pre))
    sl[d + 1] = (cot_t * sig * (1.0 + pre * (1.0 - sig))).astype(BF16)

    mine = sl.at[d + 1]

    def slope_out(n):
        return remote(mine, mine, s_send.at[n], s_recv.at[d], ((d + n) % ND, k))

    slope_out(1).start()
    slope_out(ND - 1).start()
    remote(mine, ss.at[1], n_send.at[1], n_recv.at[1], (d, sib)).start()

    @pl.when(not_first)
    def _():
        remote(mine, ss.at[2], n_send.at[0], n_recv.at[2], (d - 1, sib)).start()

    @pl.when(not_last)
    def _():
        remote(mine, ss.at[0], n_send.at[2], n_recv.at[0], (d + 1, sib)).start()

    @pl.loop(2, ND - 1)
    def _(n):
        slope_out(n).start()

    taken(ss.at[1], n_recv.at[1])

    @pl.when(not_first)
    def _():
        taken(sl.at[d], s_recv.at[d - 1])
        taken(ss.at[0], n_recv.at[0])

    @pl.when(not_last)
    def _():
        taken(sl.at[d + 2], s_recv.at[d + 1])
        taken(ss.at[2], n_recv.at[2])

    for a in (1, 0, 2):
        s = jnp.concatenate([sl[d + 2 - a], ss[2 - a]], axis=0).astype(F32)
        for cc, sc in ((1, s), (0, left(s)), (2, right(s))):
            for b, sb in ((1, sc), (0, down(sc)), (2, up(sc))):
                cm[pl.ds((a * 9 + b * 3 + cc) * O2, O2), :] = sb.astype(BF16)

    r_slot = rs.at[m]

    @pl.loop(0, 4)
    def _(q):
        rows = pl.ds(pl.multiple_of(q * 128, 128), 128)
        og[rows, :] = jnp.dot(kt[rows, :], cm[...], preferred_element_type=F32).astype(BF16)

        @pl.loop(0, 4)
        def _(i):
            j = q * 4 + i
            to = 16 * c + j
            src = og.at[pl.ds(pl.multiple_of(j * CS, CS), CS)]

            @pl.when(to != k)
            def _():
                remote(src, r_slot, r_send, r_recv, (d, to)).start()

            @pl.when(to == k)
            def _():
                pltpu.make_async_copy(src, r_slot, r_recv).start()

    @pl.loop(0, 8)
    def _(j):
        p = (j // 2) * NL + 2 * (j % 2) + c
        taken(v2.at[p], v_recv.at[p])
        remote(v2.at[p], v2.at[p], f_send, v_recv.at[p], (d, sib)).start()

    @pl.loop(0, 8)
    def _(j):
        p = (j // 2) * NL + 2 * (j % 2) + 1 - c
        taken(v2.at[p], v_recv.at[p])

    @pl.loop(0, ND)
    def _(p):
        v = v2[p].astype(F32)
        xc[p, pl.ds(0, 64), :] = right(v).astype(BF16)
        xc[p, pl.ds(64, 64), :] = v2[p]
        xc[p, pl.ds(128, 64), :] = left(v).astype(BF16)

    @pl.loop(0, ND)
    def _(p):
        @pl.when(jnp.logical_or(p < d - 1, p > d + 1))
        def _():
            taken(sl.at[p + 1], s_recv.at[p])

    @pl.loop(0, ND)
    def _(p):
        v = sl[p + 1].astype(F32)
        slb[p + 1, pl.ds(0, CS), :] = down(v).astype(BF16)
        slb[p + 1, pl.ds(CS, CS), :] = sl[p + 1]
        slb[p + 1, pl.ds(2 * CS, CS), :] = up(v).astype(BF16)

    acc[...] = jnp.zeros((9 * CS, 192), F32)

    @pl.loop(0, ND)
    def _(p):
        lhs = slb[pl.ds(p, 3)].reshape(9 * CS, VOX)
        acc[...] += lax.dot_general(
            lhs, xc[p], (((1,), (1,)), ((), ())), preferred_element_type=F32
        )

    for a in range(3):
        for b in range(3):
            rows = acc[pl.ds(((2 - a) * 3 + b) * CS, CS), :]
            for cc in range(3):
                part = rows[:, cc * 64 : cc * 64 + 64]
                kg_ref[pl.ds(a * 9 + b * 3 + cc, CS, stride=32), :] = jnp.concatenate(
                    [part, part], axis=1
                )

    taken(rs, r_recv)
    total = rs[0].astype(F32)
    for j in range(1, 16):
        total = total + rs[j].astype(F32)
    ig_ref[...] = total.T.astype(BF16)

    k_out.wait_send()
    for own, sem in ((self_a, a_send), (self_a, r_send)):
        @pl.when(own)
        def _():
            taken(xh.at[pl.ds(0, 15 * CS)], sem)

        @pl.when(jnp.logical_not(own))
        def _():
            taken(xh, sem)

    @pl.when(self_v)
    def _():
        taken(v2.at[pl.ds(0, 7)], v_send)

    @pl.when(jnp.logical_not(self_v))
    def _():
        taken(v2.at[pl.ds(0, 8)], v_send)

    taken(v2.at[pl.ds(0, 8)], f_send)
    taken(psend.at[1, 1], p_send.at[2])

    @pl.when(not_last)
    def _():
        for r in range(2):
            taken(psend.at[0, r], p_send.at[3 + r])
        taken(mine, n_send.at[2])

    @pl.when(not_first)
    def _():
        for r in range(2):
            taken(psend.at[2, r], p_send.at[5 + r])
        taken(mine, n_send.at[0])

    taken(mine, n_send.at[1])

    @pl.loop(1, ND)
    def _(n):
        taken(mine, s_send.at[n])


def local(volume, cotangent, kernel):
    any_space = pl.BlockSpec(memory_space=pl.ANY)
    in_vmem = pl.BlockSpec(memory_space=pltpu.VMEM)
    dma = pltpu.SemaphoreType.DMA
    ig, kg = pl.pallas_call(
        kernel_body,
        out_shape=(
            jax.ShapeDtypeStruct((VOX, CS), BF16),
            jax.ShapeDtypeStruct((CS * 32, 128), F32),
        ),
        in_specs=[any_space] * 3,
        out_specs=(in_vmem, in_vmem),
        scratch_shapes=[
            pltpu.VMEM((VOX, CS), BF16),
            pltpu.VMEM((VOX, CS), BF16),
            pltpu.VMEM((CS, VOX), BF16),
            pltpu.VMEM((HALF, VOX), BF16),
            pltpu.VMEM((2, CS, TAPS, HALF), BF16),
            pltpu.VMEM((4, O2 * 32, 128), F32),
            pltpu.VMEM((TPAD, HALF), BF16),
            pltpu.VMEM((HALF, TPAD), BF16),
            pltpu.VMEM((3, 2, CS, VOX), F32),
            pltpu.VMEM((3, 2, CS, VOX), F32),
            pltpu.VMEM((ND + 2, CS, VOX), BF16),
            pltpu.VMEM((3, CS, VOX), BF16),
            pltpu.VMEM((TPAD, VOX), BF16),
            pltpu.VMEM((HALF, VOX), BF16),
            pltpu.VMEM((16, CS, VOX), BF16),
            pltpu.VMEM((ND, 64, VOX), BF16),
            pltpu.VMEM((ND, 192, VOX), BF16),
            pltpu.VMEM((ND + 2, 3 * CS, VOX), BF16),
            pltpu.VMEM((9 * CS, 192), F32),
            dma((3,)), dma, dma, dma, dma, dma((7,)), dma((3, 2)), dma((ND,)), dma((ND,)),
            dma((3,)), dma((3,)), dma, dma((ND,)), dma, dma, dma,
        ],
        compiler_params=pltpu.CompilerParams(
            collective_id=0, has_side_effects=True, vmem_limit_bytes=40 * 2**20
        ),
        cost_estimate=pl.CostEstimate(
            flops=3 * 453_000_000, bytes_accessed=6_000_000, transcendentals=8192
        ),
    )(volume.reshape(VOX, CS), cotangent.reshape(VOX, CS), kernel)
    input_grad = ig.reshape(1, SIDE, SIDE, CS)
    kernel_grad = kg.reshape(1, CS, 32, 128)[:, :, :TAPS, :64]
    return (input_grad, kernel_grad)


def solution(mesh):
    return jax.shard_map(
        local,
        mesh=mesh,
        in_specs=(
            P("depth", None, None, "chan"),
            P("depth", None, None, "chan"),
            P("chan", None, None),
        ),
        out_specs=(P("depth", None, None, "chan"), P("chan", None, None, "depth")),
        check_vma=False,
    )
```

time: 499 us -> 57.6 us (0.12)
  the two profiles are of different devices: /device:TPU:8 before, /device:TPU:3 now
where the time goes in v1:
time: 57.6 us; the launch traced here: 57.5 us
  Pallas kernels  52.6 us (91%)
  local copies, waits for them, and re-layouts  4.16 us (7%)
  between operations  0.68 us (1%)
    pallas_call x1, Pallas kernels, local(): pl.pallas_call(kernel_body, out_shape=(jax.ShapeDtypeStruct((VOX, CS), BF...  52.6 us
    unnamed x7, local copies, waits for them, and re-layouts  4.16 us

profile of v1, /device:TPU:3, one launch (start us, length us, event | category | flops | bytes accessed | tf_op | source)
XLA Modules:
  0.0 57.5 jit_solution(750613663733873536)
XLA Ops:
  0.6 0.0 copy-start.1
  0.6 0.0 copy-start
  0.6 2.5 %copy.5.k_hbm = bf16[32,27,1024]{2,1,0:T(8,128)(2,1)S(1)} copy(bf16[32,27,1024]{2,0,1:T(8,128)(2,1)} %param.5) | data formatting | bytes 3538944 | tf_op args[2]
  3.2 0.0 copy-done.1
  3.2 0.0 copy-done
  3.2 52.6 %shard_map.50 = (bf16[256,32]{1,0:T(8,128)(2,1)S(1)}, f32[1024,128]{1,0:T(8,128)S(1)}) custom-call(bf16[256,32]{1,0:T(8,128)(2,1)S(1)} %bitcast.7, bf16[256,32]{1,0:T(8,128)(2,1)S(1)} %bitcast.8, bf16[32,27,1024]{2,1,0:T(8,128)(2,1)S(1)} %copy.5.k_hbm), custom_call_target="tpu_custom_call" | custom-call | flops 1359000064 | bytes 6000000 | tf_op jit(solution)/shard_map/pallas_call | solution.py:397
  55.8 1.0 %copy.7 = f32[1,32,27,64]{3,1,2,0:T(8,128)} copy(f32[1,32,27,64]{3,2,1,0:T(8,128)S(1)} %bitcast.5) | data formatting | bytes 442368
  56.8 0.6 %copy.9 = bf16[1,16,16,32]{3,2,1,0:T(8,128)(2,1)} copy(bf16[1,16,16,32]{3,2,1,0:T(8,128)(2,1)S(1)} %bitcast.6) | data formatting | bytes 32768
Async XLA Ops:
  0.6 2.5 %copy-start.1 = (bf16[1,16,16,32]{3,2,1,0:T(8,128)(2,1)S(1)}, bf16[1,16,16,32]{3,2,1,0:T(8,128)(2,1)}, u32[]{:S(2)}) copy-start(bf16[1,16,16,32]{3,2,1,0:T(8,128)(2,1)} %param.4) | copy-start | bytes 49156
  0.6 2.5 %copy-start = (bf16[1,16,16,32]{3,2,1,0:T(8,128)(2,1)S(1)}, bf16[1,16,16,32]{3,2,1,0:T(8,128)(2,1)}, u32[]{:S(2)}) copy-start(bf16[1,16,16,32]{3,2,1,0:T(8,128)(2,1)} %param.3) | copy-start | bytes 49156

commit v2 on v1

--- a/solution.py
+++ b/solution.py
@@ -15,9 +15,18 @@
 TROWS, TPAD = TAPS * O2, 28 * O2
 
 
+def finish(ig_ref, kg_ref, ig_out, kg_out, sem):
+    a = pltpu.make_async_copy(ig_ref, ig_out, sem.at[0])
+    b = pltpu.make_async_copy(kg_ref, kg_out, sem.at[1])
+    b.start()
+    a.start()
+    a.wait()
+    b.wait()
+
+
 def kernel_body(
     vol_hbm, cot_hbm, k_hbm, ig_ref, kg_ref,
-    vin, cin, xt, xh, kx, ktmp, k2, kt, psend, prec, sl, ss, cm, og, rs, v2, xc, slb, acc,
+    vin, cin, xt, xh, k2, kt, psend, prec, held, sl, ss, cm, og, rs, v2, xc, slb, acc,
     in_sem, k_send, k_recv, a_send, a_recv, p_send, p_recv, s_send, s_recv, n_send, n_recv,
     v_send, v_recv, f_send, r_send, r_recv,
 ):
@@ -41,7 +50,8 @@
     vol_in = pltpu.make_async_copy(vol_hbm, vin, in_sem.at[0])
     cot_in = pltpu.make_async_copy(cot_hbm, cin, in_sem.at[1])
     k_in = pltpu.make_async_copy(
-        k_hbm.at[:, :, pl.ds(pl.multiple_of(c * HALF, HALF), HALF)], kx.at[0], in_sem.at[2]
+        k_hbm.at[:, :, pl.ds(pl.multiple_of(c * HALF, HALF), HALF)],
+        k2.at[pl.ds(0, TAPS), pl.ds(0, CS)], in_sem.at[2],
     )
     vol_in.start()
     cot_in.start()
@@ -52,23 +62,29 @@
     def greet(dd, kk):
         pl.semaphore_signal(bar, inc=1, device_id=(dd, kk), device_id_type=MESH)
 
+    def far_first(j):
+        i = j // 2
+        dy = 4 + jnp.where(i % 2 == 1, -((i + 1) // 2), i // 2)
+        yy = (y + dy) % 8
+        return yy, yy * 2 + jnp.where(j % 2 == 0, 1 - zh, zh)
+
     @pl.loop(0, 16)
     def _(j):
-        to, frm = 2 * j + khalf, 16 * c + j
-
-        @pl.when(to != k)
-        def _():
-            greet(d, to)
-
-        @pl.when(frm != k)
-        def _():
-            greet(d, frm)
+        yy, mm = far_first(j)
+        mine = 2 * mm + khalf
+
+        @pl.when(mine != k)
+        def _():
+            greet(d, mine)
+
+        @pl.when(jnp.logical_and(yy // 4 == c, mine + 1 - 2 * khalf != k))
+        def _():
+            greet(d, mine + 1 - 2 * khalf)
 
     @pl.loop(1, ND)
     def _(j):
         greet((d + j) % ND, k)
 
-    greet(d, sib)
     greet((d + 1) % ND, sib)
     greet((d + ND - 1) % ND, sib)
     odd = (z + c) % 2
@@ -93,26 +109,26 @@
     sl[0] = zero
     sl[ND + 1] = zero
     cm[pl.ds(TROWS, O2), :] = jnp.zeros((O2, VOX), BF16)
-    k2[pl.ds(TROWS, O2), :] = jnp.zeros((O2, HALF), BF16)
+    k2[TAPS] = jnp.zeros((O2, HALF), BF16)
 
     @pl.when(d == 0)
     def _():
-        prec[0] = jnp.zeros((2, CS, VOX), F32)
+        prec[0] = jnp.zeros((2, CS, VOX), BF16)
         ss[0] = zero
 
     @pl.when(d == ND - 1)
     def _():
-        prec[2] = jnp.zeros((2, CS, VOX), F32)
+        prec[2] = jnp.zeros((2, CS, VOX), BF16)
         ss[2] = zero
 
     sa, sv = self_a.astype(jnp.int32), self_v.astype(jnp.int32)
-    pl.semaphore_wait(bar, 2 * (16 - sa) + 15 + 3 + 8 - sv)
+    pl.semaphore_wait(bar, 24 - sa + 15 + 2 + 8 - sv)
 
     a_slot = xh.at[pl.ds(pl.multiple_of((k % 16) * CS, CS), CS)]
 
     @pl.loop(0, 16)
     def _(j):
-        to = 2 * ((m + j + 8) % 16) + khalf
+        to = 2 * far_first(j)[1] + khalf
 
         @pl.when(to != k)
         def _():
@@ -123,31 +139,15 @@
             pltpu.make_async_copy(xt, a_slot, a_recv).start()
 
     k_out = remote(
-        k_hbm.at[:, :, pl.ds(pl.multiple_of((1 - c) * HALF, HALF), HALF)], kx.at[1], k_send, k_recv,
-        (d, sib),
+        k_hbm.at[:, :, pl.ds(pl.multiple_of((1 - c) * HALF, HALF), HALF)],
+        k2.at[pl.ds(0, TAPS), pl.ds(CS, CS)], k_send, k_recv, (d, sib),
     )
     k_out.start()
 
-    def widen(r):
-        @pl.loop(0, CS)
-        def _(o):
-            rows = kx[r, o].astype(F32)
-            for g in range(4):
-                ktmp[g, pl.ds(pl.multiple_of((r * CS + o) * 32, 32), TAPS), :] = rows[
-                    :, g * 128 : g * 128 + 128
-                ]
-
     k_in.wait()
-    widen(0)
     k_out.wait_recv()
-    widen(1)
-    for t in range(TAPS):
-        for g in range(4):
-            k2[pl.ds(t * O2, O2), pl.ds(g * 128, 128)] = ktmp.at[g][
-                pl.ds(t, O2, stride=32), :
-            ].astype(BF16)
     for p in range(14):
-        kt[:, pl.ds(p * 128, 128)] = k2[pl.ds(p * 128, 128), :].T
+        kt[:, pl.ds(p * 128, 128)] = k2[pl.ds(2 * p, 2)].reshape(128, HALF).T
 
     lane = lax.broadcasted_iota(jnp.int32, (1, VOX), 1)
     hh, ww = lane // SIDE, lane % SIDE
@@ -169,12 +169,11 @@
     def left(v):
         return moved(v, -1, w_hi)
 
-    cin_t = None
     taken(xh, a_recv)
     xv = xh[...]
 
     for a in (0, 2, 1):
-        yv = jnp.dot(k2[pl.ds(a * 9 * O2, 9 * O2), :], xv, preferred_element_type=F32)
+        yv = jnp.dot(k2[pl.ds(a * 9, 9)].reshape(9 * O2, HALF), xv, preferred_element_type=F32)
 
         def tap(b, cc):
             at = (b * 3 + cc) * O2
@@ -182,11 +181,13 @@
 
         cols = [tap(1, cc) + up(tap(0, cc)) + down(tap(2, cc)) for cc in range(3)]
         tot = cols[1] + right(cols[0]) + left(cols[2])
-        psend[a, 0] = tot[:CS]
-        psend[a, 1] = tot[CS:]
         if a == 1:
+            held[...] = tot[:CS]
+            psend[a, 1] = tot[CS:].astype(BF16)
             remote(psend.at[1, 1], prec.at[1, c], p_send.at[2], p_recv.at[1, c], (d, sib)).start()
         else:
+            psend[a, 0] = tot[:CS].astype(BF16)
+            psend[a, 1] = tot[CS:].astype(BF16)
             i = 0 if a == 0 else 1
             there = d + 1 - a
 
@@ -230,8 +231,8 @@
         taken(prec.at[2, 0], p_recv.at[2, 0])
         taken(prec.at[2, 1], p_recv.at[2, 1])
 
-    pre = psend[1, 0] + prec[1, 1 - c]
-    pre = pre + (prec[0, 0] + prec[0, 1]) + (prec[2, 0] + prec[2, 1])
+    got = [prec[1, 1 - c], prec[0, 0], prec[0, 1], prec[2, 0], prec[2, 1]]
+    pre = held[...] + sum(v.astype(F32) for v in got)
     sig = 1.0 / (1.0 + jnp.exp(-pre))
     sl[d + 1] = (cot_t * sig * (1.0 + pre * (1.0 - sig))).astype(BF16)
 
@@ -276,8 +277,11 @@
 
     r_slot = rs.at[m]
 
+    near = jnp.where(khalf == c, 2, 0)
+
     @pl.loop(0, 4)
-    def _(q):
+    def _(n):
+        q = (y + n + near) % 4
         rows = pl.ds(pl.multiple_of(q * 128, 128), 128)
         og[rows, :] = jnp.dot(kt[rows, :], cm[...], preferred_element_type=F32).astype(BF16)
 
@@ -295,23 +299,21 @@
             def _():
                 pltpu.make_async_copy(src, r_slot, r_recv).start()
 
-    @pl.loop(0, 8)
-    def _(j):
-        p = (j // 2) * NL + 2 * (j % 2) + c
-        taken(v2.at[p], v_recv.at[p])
-        remote(v2.at[p], v2.at[p], f_send, v_recv.at[p], (d, sib)).start()
-
-    @pl.loop(0, 8)
-    def _(j):
-        p = (j // 2) * NL + 2 * (j % 2) + 1 - c
-        taken(v2.at[p], v_recv.at[p])
-
-    @pl.loop(0, ND)
-    def _(p):
-        v = v2[p].astype(F32)
-        xc[p, pl.ds(0, 64), :] = right(v).astype(BF16)
-        xc[p, pl.ds(64, 64), :] = v2[p]
-        xc[p, pl.ds(128, 64), :] = left(v).astype(BF16)
+    def spread_chans(odd_plane, forward):
+        @pl.loop(0, 8)
+        def _(j):
+            p = (j // 2) * NL + 2 * (j % 2) + odd_plane
+            taken(v2.at[p], v_recv.at[p])
+            if forward:
+                remote(v2.at[p], v2.at[p], f_send, v_recv.at[p], (d, sib)).start()
+            v = v2[p].astype(F32)
+            xc[p, pl.ds(0, 64), :] = right(v).astype(BF16)
+            xc[p, pl.ds(64, 64), :] = v2[p]
+            xc[p, pl.ds(128, 64), :] = left(v).astype(BF16)
+
+    spread_chans(c, True)
+
+    spread_chans(1 - c, False)
 
     @pl.loop(0, ND)
     def _(p):
@@ -340,9 +342,7 @@
             rows = acc[pl.ds(((2 - a) * 3 + b) * CS, CS), :]
             for cc in range(3):
                 part = rows[:, cc * 64 : cc * 64 + 64]
-                kg_ref[pl.ds(a * 9 + b * 3 + cc, CS, stride=32), :] = jnp.concatenate(
-                    [part, part], axis=1
-                )
+                kg_ref[a * 9 + b * 3 + cc] = part
 
     taken(rs, r_recv)
     total = rs[0].astype(F32)
@@ -391,28 +391,27 @@
 
 
 def local(volume, cotangent, kernel):
-    any_space = pl.BlockSpec(memory_space=pl.ANY)
+    in_hbm = pl.BlockSpec(memory_space=pltpu.HBM)
     in_vmem = pl.BlockSpec(memory_space=pltpu.VMEM)
     dma = pltpu.SemaphoreType.DMA
     ig, kg = pl.pallas_call(
         kernel_body,
         out_shape=(
             jax.ShapeDtypeStruct((VOX, CS), BF16),
-            jax.ShapeDtypeStruct((CS * 32, 128), F32),
+            jax.ShapeDtypeStruct((TAPS, CS, 64), F32),
         ),
-        in_specs=[any_space] * 3,
+        in_specs=[in_hbm] * 3,
         out_specs=(in_vmem, in_vmem),
         scratch_shapes=[
             pltpu.VMEM((VOX, CS), BF16),
             pltpu.VMEM((VOX, CS), BF16),
             pltpu.VMEM((CS, VOX), BF16),
             pltpu.VMEM((HALF, VOX), BF16),
-            pltpu.VMEM((2, CS, TAPS, HALF), BF16),
-            pltpu.VMEM((4, O2 * 32, 128), F32),
-            pltpu.VMEM((TPAD, HALF), BF16),
+                    pltpu.VMEM((28, O2, HALF), BF16),
             pltpu.VMEM((HALF, TPAD), BF16),
-            pltpu.VMEM((3, 2, CS, VOX), F32),
-            pltpu.VMEM((3, 2, CS, VOX), F32),
+            pltpu.VMEM((3, 2, CS, VOX), BF16),
+            pltpu.VMEM((3, 2, CS, VOX), BF16),
+            pltpu.VMEM((CS, VOX), F32),
             pltpu.VMEM((ND + 2, CS, VOX), BF16),
             pltpu.VMEM((3, CS, VOX), BF16),
             pltpu.VMEM((TPAD, VOX), BF16),
@@ -426,14 +425,28 @@
             dma((3,)), dma((3,)), dma, dma((ND,)), dma, dma, dma,
         ],
         compiler_params=pltpu.CompilerParams(
-            collective_id=0, has_side_effects=True, vmem_limit_bytes=40 * 2**20
+            collective_id=0, has_side_effects=True, vmem_limit_bytes=48 * 2**20
         ),
         cost_estimate=pl.CostEstimate(
             flops=3 * 453_000_000, bytes_accessed=6_000_000, transcendentals=8192
         ),
-    )(volume.reshape(VOX, CS), cotangent.reshape(VOX, CS), kernel)
+    )(
+        pltpu.with_memory_space_constraint(volume.reshape(VOX, CS), pltpu.HBM),
+        pltpu.with_memory_space_constraint(cotangent.reshape(VOX, CS), pltpu.HBM),
+        pltpu.with_memory_space_constraint(jnp.transpose(kernel, (1, 0, 2)), pltpu.HBM),
+    )
+    ig, kg = pl.pallas_call(
+        finish,
+        out_shape=(
+            jax.ShapeDtypeStruct((VOX, CS), BF16),
+            jax.ShapeDtypeStruct((TAPS, CS, 64), F32),
+        ),
+        in_specs=[pl.BlockSpec(memory_space=pl.ANY)] * 2,
+        out_specs=(pl.BlockSpec(memory_space=pl.ANY),) * 2,
+        scratch_shapes=[dma((2,))],
+    )(*(pltpu.with_memory_space_constraint(v, pltpu.VMEM) for v in (ig, kg)))
     input_grad = ig.reshape(1, SIDE, SIDE, CS)
-    kernel_grad = kg.reshape(1, CS, 32, 128)[:, :, :TAPS, :64]
+    kernel_grad = jnp.transpose(kg, (1, 0, 2))[None]
     return (input_grad, kernel_grad)
 
 

time: 57.6 us -> 50.5 us (0.88)
  the two profiles are of different devices: /device:TPU:3 before, /device:TPU:13 now
where the time goes in v2:
time: 50.5 us; the launch traced here: 50.4 us
  Pallas kernels  49.8 us (99%)
  between operations  0.64 us (1%)
    pallas_call x1, Pallas kernels, local(): pl.pallas_call(kernel_body, out_shape=(jax.ShapeDtypeStruct((VOX, CS), BF...  49 us

profile of v2, /device:TPU:13, one launch (start us, length us, event | category | flops | bytes accessed | tf_op | source)
XLA Modules:
  0.0 50.4 jit_solution(10511021865029950113)
XLA Ops:
  0.6 49.0 %shard_map.50 = (bf16[256,32]{1,0:T(8,128)(2,1)S(1)}, f32[27,32,64]{2,1,0:T(8,128)S(1)}) custom-call(bf16[256,32]{1,0:T(8,128)(2,1)} %bitcast.9, bf16[256,32]{1,0:T(8,128)(2,1)} %bitcast.10, bf16[27,32,1024]{2,1,0:T(8,128)(2,1)} %bitcast.7), custom_call_target="tpu_custom_call" | custom-call | flops 1359000064 | bytes 6000000 | tf_op jit(solution)/shard_map/pallas_call | solution.py:397
  49.6 0.8 %shard_map.51 = (bf16[256,32]{1,0:T(8,128)(2,1)}, f32[27,32,64]{2,1,0:T(8,128)}) custom-call(bf16[256,32]{1,0:T(8,128)(2,1)S(1)} %get-tuple-element.6.ig_ref, f32[27,32,64]{2,1,0:T(8,128)S(1)} %get-tuple-element.7.kg_ref), custom_call_target="tpu_custom_call" | custom-call | tf_op jit(solution)/shard_map/pallas_call | solution.py:438

commit v3 on v2

--- a/solution.py
+++ b/solution.py
@@ -63,10 +63,10 @@
         pl.semaphore_signal(bar, inc=1, device_id=(dd, kk), device_id_type=MESH)
 
     def far_first(j):
-        i = j // 2
+        i = j % 8
         dy = 4 + jnp.where(i % 2 == 1, -((i + 1) // 2), i // 2)
         yy = (y + dy) % 8
-        return yy, yy * 2 + jnp.where(j % 2 == 0, 1 - zh, zh)
+        return yy, yy * 2 + jnp.where(j < 8, 1 - zh, zh)
 
     @pl.loop(0, 16)
     def _(j):
@@ -201,11 +201,11 @@
 
     @pl.loop(0, 8)
     def _(j):
-        xd, t = 2 * c + j // 4, j % 4
-        step = jnp.where(t == 3, 2 - 4 * (x % 2), t - 1)
+        xd, t = 2 * c + j % 2, j // 2
+        step = jnp.where(t == 0, 2 - 4 * (x % 2), jnp.where(t == 3, 0, 2 * t - 3))
         zd = (z + step + NZ) % NZ
         dd, kk = xd * NL + zd % NL, (y * 2 + zd // NL) * 2 + zl % 2
-        src = xh.at[pl.ds(pl.multiple_of(((j // 4) * NL + zd % NL) * 64, 64), 64)]
+        src = xh.at[pl.ds(pl.multiple_of(((j % 2) * NL + zd % NL) * 64, 64), 64)]
         own = jnp.logical_and(dd == d, kk == k)
 
         @pl.when(jnp.logical_not(own))
@@ -277,17 +277,20 @@
 
     r_slot = rs.at[m]
 
-    near = jnp.where(khalf == c, 2, 0)
-
-    @pl.loop(0, 4)
+    @pl.loop(0, 2)
     def _(n):
-        q = (y + n + near) % 4
-        rows = pl.ds(pl.multiple_of(q * 128, 128), 128)
-        og[rows, :] = jnp.dot(kt[rows, :], cm[...], preferred_element_type=F32).astype(BF16)
-
-        @pl.loop(0, 4)
+        zd = jnp.where(n == 0, 1 - zh, zh)
+        lhs = jnp.concatenate(
+            [kt[pl.ds(pl.multiple_of(i * 128 + zd * 64, 64), 64), :] for i in range(4)], axis=0
+        )
+        part = jnp.dot(lhs, cm[...], preferred_element_type=F32).astype(BF16)
+        for i in range(4):
+            og[pl.ds(pl.multiple_of(i * 128 + zd * 64, 64), 64), :] = part[i * 64 : i * 64 + 64]
+
+        @pl.loop(0, 8)
         def _(i):
-            j = q * 4 + i
+            far = (y + i // 2 + jnp.where(khalf == c, 2, 0)) % 4
+            j = far * 4 + zd * 2 + i % 2
             to = 16 * c + j
             src = og.at[pl.ds(pl.multiple_of(j * CS, CS), CS)]
 
@@ -300,7 +303,7 @@
                 pltpu.make_async_copy(src, r_slot, r_recv).start()
 
     def spread_chans(odd_plane, forward):
-        @pl.loop(0, 8)
+        @pl.loop(0, 8, unroll=2)
         def _(j):
             p = (j // 2) * NL + 2 * (j % 2) + odd_plane
             taken(v2.at[p], v_recv.at[p])
@@ -321,21 +324,20 @@
         def _():
             taken(sl.at[p + 1], s_recv.at[p])
 
-    @pl.loop(0, ND)
+    @pl.loop(0, ND, unroll=4)
     def _(p):
         v = sl[p + 1].astype(F32)
         slb[p + 1, pl.ds(0, CS), :] = down(v).astype(BF16)
         slb[p + 1, pl.ds(CS, CS), :] = sl[p + 1]
         slb[p + 1, pl.ds(2 * CS, CS), :] = up(v).astype(BF16)
 
-    acc[...] = jnp.zeros((9 * CS, 192), F32)
-
-    @pl.loop(0, ND)
-    def _(p):
-        lhs = slb[pl.ds(p, 3)].reshape(9 * CS, VOX)
-        acc[...] += lax.dot_general(
-            lhs, xc[p], (((1,), (1,)), ((), ())), preferred_element_type=F32
+    for p in range(0, ND, 4):
+        lhs = jnp.concatenate(
+            [slb[pl.ds(p + i, 3)].reshape(9 * CS, VOX) for i in range(4)], axis=1
         )
+        rhs = jnp.concatenate([xc[p + i] for i in range(4)], axis=1)
+        part = lax.dot_general(lhs, rhs, (((1,), (1,)), ((), ())), preferred_element_type=F32)
+        acc[...] = part if p == 0 else acc[...] + part
 
     for a in range(3):
         for b in range(3):

time: 50.5 us -> 48.3 us (0.956)
  the two profiles are of different devices: /device:TPU:13 before, /device:TPU:5 now
where the time goes in v3:
time: 48.3 us; the launch traced here: 48.2 us
  Pallas kernels  47.5 us (98%)
  between operations  0.64 us (1%)
    pallas_call x1, Pallas kernels, local(): pl.pallas_call(kernel_body, out_shape=(jax.ShapeDtypeStruct((VOX, CS), BF...  46.8 us

profile of v3, /device:TPU:5, one launch (start us, length us, event | category | flops | bytes accessed | tf_op | source)
XLA Modules:
  0.0 48.2 jit_solution(8619008752178701618)
XLA Ops:
  0.6 46.8 %shard_map.50 = (bf16[256,32]{1,0:T(8,128)(2,1)S(1)}, f32[27,32,64]{2,1,0:T(8,128)S(1)}) custom-call(bf16[256,32]{1,0:T(8,128)(2,1)} %bitcast.9, bf16[256,32]{1,0:T(8,128)(2,1)} %bitcast.10, bf16[27,32,1024]{2,1,0:T(8,128)(2,1)} %bitcast.7), custom_call_target="tpu_custom_call" | custom-call | flops 1359000064 | bytes 6000000 | tf_op jit(solution)/shard_map/pallas_call | solution.py:399
  47.4 0.8 %shard_map.51 = (bf16[256,32]{1,0:T(8,128)(2,1)}, f32[27,32,64]{2,1,0:T(8,128)}) custom-call(bf16[256,32]{1,0:T(8,128)(2,1)S(1)} %get-tuple-element.6.ig_ref, f32[27,32,64]{2,1,0:T(8,128)S(1)} %get-tuple-element.7.kg_ref), custom_call_target="tpu_custom_call" | custom-call | tf_op jit(solution)/shard_map/pallas_call | solution.py:440

commit v4 on v3

--- a/solution.py
+++ b/solution.py
@@ -81,12 +81,15 @@
         def _():
             greet(d, mine + 1 - 2 * khalf)
 
-    @pl.loop(1, ND)
+    @pl.loop(1, 4)
     def _(j):
-        greet((d + j) % ND, k)
-
-    greet((d + 1) % ND, sib)
-    greet((d + ND - 1) % ND, sib)
+        greet((x + j) % NX * NL + zl, k)
+        greet(x * NL + (zl + j) % NL, k)
+
+    for kk in (k, sib):
+        greet((d + 1) % ND, kk)
+        greet((d + ND - 1) % ND, kk)
+
     odd = (z + c) % 2
 
     @pl.loop(0, 8)
@@ -122,7 +125,7 @@
         ss[2] = zero
 
     sa, sv = self_a.astype(jnp.int32), self_v.astype(jnp.int32)
-    pl.semaphore_wait(bar, 24 - sa + 15 + 2 + 8 - sv)
+    pl.semaphore_wait(bar, 24 - sa + 6 + 4 + 8 - sv)
 
     a_slot = xh.at[pl.ds(pl.multiple_of((k % 16) * CS, CS), CS)]
 
@@ -132,11 +135,11 @@
 
         @pl.when(to != k)
         def _():
-            remote(xt, a_slot, a_send, a_recv, (d, to)).start()
+            remote(xt, a_slot, a_send, a_recv.at[zh], (d, to)).start()
 
         @pl.when(to == k)
         def _():
-            pltpu.make_async_copy(xt, a_slot, a_recv).start()
+            pltpu.make_async_copy(xt, a_slot, a_recv.at[zh]).start()
 
     k_out = remote(
         k_hbm.at[:, :, pl.ds(pl.multiple_of((1 - c) * HALF, HALF), HALF)],
@@ -169,7 +172,28 @@
     def left(v):
         return moved(v, -1, w_hi)
 
-    taken(xh, a_recv)
+    def spread_out(other):
+      @pl.loop(0, 4)
+      def _(j):
+        xd, t = 2 * c + j % 2, j // 2
+        even = (z + zh + other) % 2 == 0
+        step = jnp.where(even, (1 - t) * (2 - 4 * (x % 2)), 2 * t - 1)
+        zd = (z + step + NZ) % NZ
+        dd, kk = xd * NL + zd % NL, (y * 2 + zd // NL) * 2 + zl % 2
+        src = xh.at[pl.ds(pl.multiple_of(((j % 2) * NL + zd % NL) * 64, 64), 64)]
+        own = jnp.logical_and(dd == d, kk == k)
+
+        @pl.when(jnp.logical_not(own))
+        def _():
+            remote(src, v2.at[d], v_send, v_recv.at[d], (dd, kk)).start()
+
+        @pl.when(own)
+        def _():
+            pltpu.make_async_copy(src, v2.at[d], v_recv.at[d]).start()
+
+    taken(xh.at[pl.ds(0, 8 * CS)], a_recv.at[zh])
+    spread_out(0)
+    taken(xh.at[pl.ds(0, 8 * CS)], a_recv.at[1 - zh])
     xv = xh[...]
 
     for a in (0, 2, 1):
@@ -199,22 +223,7 @@
                         (there, kk),
                     ).start()
 
-    @pl.loop(0, 8)
-    def _(j):
-        xd, t = 2 * c + j % 2, j // 2
-        step = jnp.where(t == 0, 2 - 4 * (x % 2), jnp.where(t == 3, 0, 2 * t - 3))
-        zd = (z + step + NZ) % NZ
-        dd, kk = xd * NL + zd % NL, (y * 2 + zd // NL) * 2 + zl % 2
-        src = xh.at[pl.ds(pl.multiple_of(((j % 2) * NL + zd % NL) * 64, 64), 64)]
-        own = jnp.logical_and(dd == d, kk == k)
-
-        @pl.when(jnp.logical_not(own))
-        def _():
-            remote(src, v2.at[d], v_send, v_recv.at[d], (dd, kk)).start()
-
-        @pl.when(own)
-        def _():
-            pltpu.make_async_copy(src, v2.at[d], v_recv.at[d]).start()
+    spread_out(1)
 
     cot_in.wait()
     cot_t = cin[...].astype(F32).T
@@ -238,11 +247,59 @@
 
     mine = sl.at[d + 1]
 
-    def slope_out(n):
-        return remote(mine, mine, s_send.at[n], s_recv.at[d], ((d + n) % ND, k))
-
-    slope_out(1).start()
-    slope_out(ND - 1).start()
+    def slope_out(plane, to, i):
+        at = sl.at[plane + 1]
+        return remote(at, at, s_send.at[i], s_recv.at[plane], (to, k))
+
+    far_up, far_down = jnp.logical_and(zl == 3, not_last), jnp.logical_and(zl == 0, not_first)
+
+    def own_copies(act):
+        @pl.when(far_up)
+        def _():
+            act(d, d + 1, 8)
+
+        @pl.when(far_down)
+        def _():
+            act(d, d - 1, 9)
+
+        @pl.loop(0, NL)
+        def _(t):
+            @pl.when(t != zl)
+            def _():
+                act(d, x * NL + t, t)
+
+    def own_along_x(act):
+        @pl.loop(0, NX)
+        def _(t):
+            @pl.when(t != x)
+            def _():
+                act(d, t * NL + zl, 4 + t)
+
+    def passed_on(act, first):
+        @pl.loop(0, NL)
+        def _(zs):
+            p = x * NL + zs
+
+            @pl.when(zs != zl)
+            def _():
+                first(p)
+
+                @pl.loop(0, NX)
+                def _(t):
+                    to = t * NL + zl
+                    near = jnp.logical_or(to == p + 1, to == p - 1)
+
+                    @pl.when(jnp.logical_and(t != x, jnp.logical_not(near)))
+                    def _():
+                        act(p, to, 16 + zs * NX + t)
+
+    def send(plane, to, i):
+        slope_out(plane, to, i).start()
+
+    def sent(plane, to, i):
+        taken(mine, s_send.at[i])
+
+    own_copies(send)
     remote(mine, ss.at[1], n_send.at[1], n_recv.at[1], (d, sib)).start()
 
     @pl.when(not_first)
@@ -253,27 +310,29 @@
     def _():
         remote(mine, ss.at[0], n_send.at[2], n_recv.at[0], (d + 1, sib)).start()
 
-    @pl.loop(2, ND - 1)
-    def _(n):
-        slope_out(n).start()
-
-    taken(ss.at[1], n_recv.at[1])
-
-    @pl.when(not_first)
-    def _():
-        taken(sl.at[d], s_recv.at[d - 1])
-        taken(ss.at[0], n_recv.at[0])
-
-    @pl.when(not_last)
-    def _():
-        taken(sl.at[d + 2], s_recv.at[d + 1])
-        taken(ss.at[2], n_recv.at[2])
-
-    for a in (1, 0, 2):
+    own_along_x(send)
+
+    def columns(a):
         s = jnp.concatenate([sl[d + 2 - a], ss[2 - a]], axis=0).astype(F32)
         for cc, sc in ((1, s), (0, left(s)), (2, right(s))):
             for b, sb in ((1, sc), (0, down(sc)), (2, up(sc))):
                 cm[pl.ds((a * 9 + b * 3 + cc) * O2, O2), :] = sb.astype(BF16)
+
+    taken(ss.at[1], n_recv.at[1])
+    columns(1)
+
+    @pl.when(not_first)
+    def _():
+        taken(sl.at[d], s_recv.at[d - 1])
+        taken(ss.at[0], n_recv.at[0])
+
+    @pl.when(not_last)
+    def _():
+        taken(sl.at[d + 2], s_recv.at[d + 1])
+        taken(ss.at[2], n_recv.at[2])
+
+    columns(0)
+    columns(2)
 
     r_slot = rs.at[m]
 
@@ -301,6 +360,13 @@
             @pl.when(to == k)
             def _():
                 pltpu.make_async_copy(src, r_slot, r_recv).start()
+
+    def arrived(p):
+        @pl.when(jnp.logical_or(p < d - 1, p > d + 1))
+        def _():
+            taken(sl.at[p + 1], s_recv.at[p])
+
+    passed_on(send, arrived)
 
     def spread_chans(odd_plane, forward):
         @pl.loop(0, 8, unroll=2)
@@ -320,9 +386,9 @@
 
     @pl.loop(0, ND)
     def _(p):
-        @pl.when(jnp.logical_or(p < d - 1, p > d + 1))
-        def _():
-            taken(sl.at[p + 1], s_recv.at[p])
+        @pl.when(p // NL != x)
+        def _():
+            arrived(p)
 
     @pl.loop(0, ND, unroll=4)
     def _(p):
@@ -346,50 +412,50 @@
                 part = rows[:, cc * 64 : cc * 64 + 64]
                 kg_ref[a * 9 + b * 3 + cc] = part
 
+    k_out.wait_send()
+    for own, sem in ((self_a, a_send), (self_a, r_send)):
+        @pl.when(own)
+        def _():
+            taken(xh.at[pl.ds(0, 15 * CS)], sem)
+
+        @pl.when(jnp.logical_not(own))
+        def _():
+            taken(xh, sem)
+
+    @pl.when(self_v)
+    def _():
+        taken(v2.at[pl.ds(0, 7)], v_send)
+
+    @pl.when(jnp.logical_not(self_v))
+    def _():
+        taken(v2.at[pl.ds(0, 8)], v_send)
+
+    taken(v2.at[pl.ds(0, 8)], f_send)
+    taken(psend.at[1, 1], p_send.at[2])
+
+    @pl.when(not_last)
+    def _():
+        for r in range(2):
+            taken(psend.at[0, r], p_send.at[3 + r])
+        taken(mine, n_send.at[2])
+
+    @pl.when(not_first)
+    def _():
+        for r in range(2):
+            taken(psend.at[2, r], p_send.at[5 + r])
+        taken(mine, n_send.at[0])
+
+    taken(mine, n_send.at[1])
+
+    own_copies(sent)
+    own_along_x(sent)
+    passed_on(sent, lambda p: None)
+
     taken(rs, r_recv)
     total = rs[0].astype(F32)
     for j in range(1, 16):
         total = total + rs[j].astype(F32)
     ig_ref[...] = total.T.astype(BF16)
-
-    k_out.wait_send()
-    for own, sem in ((self_a, a_send), (self_a, r_send)):
-        @pl.when(own)
-        def _():
-            taken(xh.at[pl.ds(0, 15 * CS)], sem)
-
-        @pl.when(jnp.logical_not(own))
-        def _():
-            taken(xh, sem)
-
-    @pl.when(self_v)
-    def _():
-        taken(v2.at[pl.ds(0, 7)], v_send)
-
-    @pl.when(jnp.logical_not(self_v))
-    def _():
-        taken(v2.at[pl.ds(0, 8)], v_send)
-
-    taken(v2.at[pl.ds(0, 8)], f_send)
-    taken(psend.at[1, 1], p_send.at[2])
-
-    @pl.when(not_last)
-    def _():
-        for r in range(2):
-            taken(psend.at[0, r], p_send.at[3 + r])
-        taken(mine, n_send.at[2])
-
-    @pl.when(not_first)
-    def _():
-        for r in range(2):
-            taken(psend.at[2, r], p_send.at[5 + r])
-        taken(mine, n_send.at[0])
-
-    taken(mine, n_send.at[1])
-
-    @pl.loop(1, ND)
-    def _(n):
-        taken(mine, s_send.at[n])
 
 
 def local(volume, cotangent, kernel):
@@ -423,7 +489,7 @@
             pltpu.VMEM((ND, 192, VOX), BF16),
             pltpu.VMEM((ND + 2, 3 * CS, VOX), BF16),
             pltpu.VMEM((9 * CS, 192), F32),
-            dma((3,)), dma, dma, dma, dma, dma((7,)), dma((3, 2)), dma((ND,)), dma((ND,)),
+            dma((3,)), dma, dma, dma, dma((2,)), dma((7,)), dma((3, 2)), dma((32,)), dma((ND,)),
             dma((3,)), dma((3,)), dma, dma((ND,)), dma, dma, dma,
         ],
         compiler_params=pltpu.CompilerParams(

time: 48.3 us -> 48 us (level)
  the two profiles are of different devices: /device:TPU:5 before, /device:TPU:11 now
where the time goes in v4:
time: 48 us; the launch traced here: 47.9 us
  Pallas kernels  47.3 us (99%)
  between operations  0.64 us (1%)
    pallas_call x1, Pallas kernels, local(): pl.pallas_call(kernel_body, out_shape=(jax.ShapeDtypeStruct((VOX, CS), BF...  46.5 us

profile of v4, /device:TPU:11, one launch (start us, length us, event | category | flops | bytes accessed | tf_op | source)
XLA Modules:
  0.0 47.9 jit_solution(5745705605786793)
XLA Ops:
  0.6 46.5 %shard_map.50 = (bf16[256,32]{1,0:T(8,128)(2,1)S(1)}, f32[27,32,64]{2,1,0:T(8,128)S(1)}) custom-call(bf16[256,32]{1,0:T(8,128)(2,1)} %bitcast.9, bf16[256,32]{1,0:T(8,128)(2,1)} %bitcast.10, bf16[27,32,1024]{2,1,0:T(8,128)(2,1)} %bitcast.7), custom_call_target="tpu_custom_call" | custom-call | flops 1359000064 | bytes 6000000 | tf_op jit(solution)/shard_map/pallas_call | solution.py:465
  47.1 0.8 %shard_map.51 = (bf16[256,32]{1,0:T(8,128)(2,1)}, f32[27,32,64]{2,1,0:T(8,128)}) custom-call(bf16[256,32]{1,0:T(8,128)(2,1)S(1)} %get-tuple-element.6.ig_ref, f32[27,32,64]{2,1,0:T(8,128)S(1)} %get-tuple-element.7.kg_ref), custom_call_target="tpu_custom_call" | custom-call | tf_op jit(solution)/shard_map/pallas_call | solution.py:506

commit v5 on v4

--- a/solution.py
+++ b/solution.py
@@ -262,13 +262,21 @@
         def _():
             act(d, d - 1, 9)
 
+        @pl.when(zl < NL - 1)
+        def _():
+            act(d, d + 1, zl + 1)
+
+        @pl.when(zl > 0)
+        def _():
+            act(d, d - 1, zl - 1)
+
+    def own_along(act):
         @pl.loop(0, NL)
         def _(t):
-            @pl.when(t != zl)
+            @pl.when(jnp.logical_or(t < zl - 1, t > zl + 1))
             def _():
                 act(d, x * NL + t, t)
 
-    def own_along_x(act):
         @pl.loop(0, NX)
         def _(t):
             @pl.when(t != x)
@@ -310,7 +318,7 @@
     def _():
         remote(mine, ss.at[0], n_send.at[2], n_recv.at[0], (d + 1, sib)).start()
 
-    own_along_x(send)
+    own_along(send)
 
     def columns(a):
         s = jnp.concatenate([sl[d + 2 - a], ss[2 - a]], axis=0).astype(F32)
@@ -448,7 +456,7 @@
     taken(mine, n_send.at[1])
 
     own_copies(sent)
-    own_along_x(sent)
+    own_along(sent)
     passed_on(sent, lambda p: None)
 
     taken(rs, r_recv)

time: 48 us -> 47.5 us (0.990)
  the two profiles are of different devices: /device:TPU:11 before, /device:TPU:5 now
where the time goes in v5:
time: 47.5 us; the launch traced here: 47.2 us
  Pallas kernels  46.6 us (98%)
  between operations  0.64 us (1%)
    pallas_call x1, Pallas kernels, local(): pl.pallas_call(kernel_body, out_shape=(jax.ShapeDtypeStruct((VOX, CS), BF...  45.8 us

profile of v5, /device:TPU:5, one launch (start us, length us, event | category | flops | bytes accessed | tf_op | source)
XLA Modules:
  0.0 47.2 jit_solution(11976267552574335517)
XLA Ops:
  0.6 45.8 %shard_map.50 = (bf16[256,32]{1,0:T(8,128)(2,1)S(1)}, f32[27,32,64]{2,1,0:T(8,128)S(1)}) custom-call(bf16[256,32]{1,0:T(8,128)(2,1)} %bitcast.9, bf16[256,32]{1,0:T(8,128)(2,1)} %bitcast.10, bf16[27,32,1024]{2,1,0:T(8,128)(2,1)} %bitcast.7), custom_call_target="tpu_custom_call" | custom-call | flops 1359000064 | bytes 6000000 | tf_op jit(solution)/shard_map/pallas_call | solution.py:473
  46.4 0.8 %shard_map.51 = (bf16[256,32]{1,0:T(8,128)(2,1)}, f32[27,32,64]{2,1,0:T(8,128)}) custom-call(bf16[256,32]{1,0:T(8,128)(2,1)S(1)} %get-tuple-element.6.ig_ref, f32[27,32,64]{2,1,0:T(8,128)S(1)} %get-tuple-element.7.kg_ref), custom_call_target="tpu_custom_call" | custom-call | tf_op jit(solution)/shard_map/pallas_call | solution.py:514

commit v6 on v5

--- a/solution.py
+++ b/solution.py
@@ -318,8 +318,6 @@
     def _():
         remote(mine, ss.at[0], n_send.at[2], n_recv.at[0], (d + 1, sib)).start()
 
-    own_along(send)
-
     def columns(a):
         s = jnp.concatenate([sl[d + 2 - a], ss[2 - a]], axis=0).astype(F32)
         for cc, sc in ((1, s), (0, left(s)), (2, right(s))):
@@ -328,6 +326,7 @@
 
     taken(ss.at[1], n_recv.at[1])
     columns(1)
+    own_along(send)
 
     @pl.when(not_first)
     def _():

time: 47.5 us -> 47.3 us (level)
  no operation moved by 1% of the time
where the time goes in v6:
time: 47.3 us; the launch traced here: 47.1 us
  Pallas kernels  46.5 us (98%)
  between operations  0.64 us (1%)
    pallas_call x1, Pallas kernels, local(): pl.pallas_call(kernel_body, out_shape=(jax.ShapeDtypeStruct((VOX, CS), BF...  45.7 us

profile of v6, /device:TPU:5, one launch (start us, length us, event | category | flops | bytes accessed | tf_op | source)
XLA Modules:
  0.0 47.1 jit_solution(17321649495366684745)
XLA Ops:
  0.6 45.7 %shard_map.50 = (bf16[256,32]{1,0:T(8,128)(2,1)S(1)}, f32[27,32,64]{2,1,0:T(8,128)S(1)}) custom-call(bf16[256,32]{1,0:T(8,128)(2,1)} %bitcast.9, bf16[256,32]{1,0:T(8,128)(2,1)} %bitcast.10, bf16[27,32,1024]{2,1,0:T(8,128)(2,1)} %bitcast.7), custom_call_target="tpu_custom_call" | custom-call | flops 1359000064 | bytes 6000000 | tf_op jit(solution)/shard_map/pallas_call | solution.py:472
  46.4 0.8 %shard_map.51 = (bf16[256,32]{1,0:T(8,128)(2,1)}, f32[27,32,64]{2,1,0:T(8,128)}) custom-call(bf16[256,32]{1,0:T(8,128)(2,1)S(1)} %get-tuple-element.6.ig_ref, f32[27,32,64]{2,1,0:T(8,128)S(1)} %get-tuple-element.7.kg_ref), custom_call_target="tpu_custom_call" | custom-call | tf_op jit(solution)/shard_map/pallas_call | solution.py:513

commit v7 on v6

--- a/solution.py
+++ b/solution.py
@@ -326,7 +326,6 @@
 
     taken(ss.at[1], n_recv.at[1])
     columns(1)
-    own_along(send)
 
     @pl.when(not_first)
     def _():
@@ -338,6 +337,7 @@
         taken(sl.at[d + 2], s_recv.at[d + 1])
         taken(ss.at[2], n_recv.at[2])
 
+    own_along(send)
     columns(0)
     columns(2)
 

time: 47.3 us -> 48.9 us (1.034)
  the two profiles are of different devices: /device:TPU:5 before, /device:TPU:54 now
where the time goes in v7:
time: 48.9 us; the launch traced here: 48.8 us
  Pallas kernels  48.2 us (99%)
  between operations  0.64 us (1%)
    pallas_call x1, Pallas kernels, local(): pl.pallas_call(kernel_body, out_shape=(jax.ShapeDtypeStruct((VOX, CS), BF...  47.4 us

profile of v7, /device:TPU:54, one launch (start us, length us, event | category | flops | bytes accessed | tf_op | source)
XLA Modules:
  0.0 48.8 jit_solution(16967928279768950939)
XLA Ops:
  0.6 47.4 %shard_map.50 = (bf16[256,32]{1,0:T(8,128)(2,1)S(1)}, f32[27,32,64]{2,1,0:T(8,128)S(1)}) custom-call(bf16[256,32]{1,0:T(8,128)(2,1)} %bitcast.9, bf16[256,32]{1,0:T(8,128)(2,1)} %bitcast.10, bf16[27,32,1024]{2,1,0:T(8,128)(2,1)} %bitcast.7), custom_call_target="tpu_custom_call" | custom-call | flops 1359000064 | bytes 6000000 | tf_op jit(solution)/shard_map/pallas_call | solution.py:472
  48.0 0.8 %shard_map.51 = (bf16[256,32]{1,0:T(8,128)(2,1)}, f32[27,32,64]{2,1,0:T(8,128)}) custom-call(bf16[256,32]{1,0:T(8,128)(2,1)S(1)} %get-tuple-element.6.ig_ref, f32[27,32,64]{2,1,0:T(8,128)S(1)} %get-tuple-element.7.kg_ref), custom_call_target="tpu_custom_call" | custom-call | tf_op jit(solution)/shard_map/pallas_call | solution.py:513
